TPU v7x, 512 devices: a whole 4x8x8 slice. The times are simulated.
512 devices in a mesh: node: 32 (over x, y), chan: 16 (over z, core).
Axes of the slice: x: 4, y: 8, z: 8, core: 2. Of those that a mesh axis runs over, the one named last changes fastest.
Arguments:
- features: bfloat16 [57344, 1024], P('node', 'chan'), may hold values from -0.046875 to 0.046875
- weight: bfloat16 [1024, 1024], P('node', 'chan'), may hold values from -0.375 to 0.375
- pre_clean: bfloat16 [57344, 1024], P('node', 'chan'), may hold values from -6 to 6
- pre_corrupt: bfloat16 [57344, 1024], P('node', 'chan'), may hold values from -6 to 6
- grad_clean: bfloat16 [57344, 1024], P('node', 'chan'), may hold values from -6 to 6
- grad_corrupt: bfloat16 [57344, 1024], P('node', 'chan'), may hold values from -6 to 6
- slopes: float32 [1024], P('chan'), may hold values from 0.05 to 0.5
- adj_vals: bfloat16 [448, 5, 128, 128], P('node'), may hold values from 0 to 0.07861328
- adj_cols: int32 [448, 5], P('node'), may hold values from 0 to 447, as said below
- adj_count: int32 [448], P('node'), may hold values from 1 to 5, as said below
- shuffle_from: int32 [448], replicated, may hold values from 0 to 447, as said below
Outputs:
- grad_weight: float32 [1024, 1024], P('node', 'chan')
- grad_features: bfloat16 [57344, 1024], P('node', 'chan')
Inputs may be any that keep to these rules, and one draw needn't show every extreme that they name: `adj_cols`: entry [b, k] is a block within 2 of b, and entry [b, 0] is b itself. Slots k < adj_count[b] of row block b hold edge tiles; the other slots are padding and are not read. `shuffle_from`: A permutation of the blocks. The 14 blocks of one index of node take their rows from exactly 14 distinct indices of node, 1 block from each; among these are the index just after it and the index 16 away, counted round.
All inputs are finite; a program needn't handle non-finite values.
Results may differ from a plain program's by a relative error of at most 0.023.
Values may be sent and summed in bfloat16 or wider, within the bound.
A program may use at most 64 MiB of HBM per device.

v0:
```python
import jax
import jax.numpy as jnp
from jax import lax
from jax.sharding import PartitionSpec as P


def shifted(value, axis, by):
    size = lax.axis_size(axis)
    pairs = [(i, i + by) for i in range(size) if 0 <= i + by < size]
    return lax.ppermute(value, axis, pairs)


def local_grad(grad_part, pre_part, slopes):
    factor = jnp.where(pre_part > 0, 1.0, slopes[None, :])
    return (grad_part.astype(jnp.float32) * factor).astype(jnp.bfloat16)


def local(
    features,
    weight,
    pre_clean,
    pre_corrupt,
    grad_clean,
    grad_corrupt,
    slopes,
    adj_vals,
    adj_cols,
    adj_count,
    shuffle_from,
):
    row_count, chan_width = features.shape
    blocks = adj_vals.shape[0]
    tile_slots = adj_vals.shape[1]
    tile_rows = adj_vals.shape[2]
    band_reach = (tile_slots - 1) // 2
    my_index = lax.axis_index("node")
    dev_count = lax.axis_size("node")
    d_clean = local_grad(grad_clean, pre_clean, slopes)
    d_corrupt = local_grad(grad_corrupt, pre_corrupt, slopes)
    stacked = jnp.concatenate([d_clean, d_corrupt], axis=1).reshape(
        blocks, tile_rows, 2 * chan_width
    )
    contrib = jnp.einsum("bkpq,bpc->bkqc", adj_vals, stacked, preferred_element_type=jnp.float32)
    span_blocks = blocks + 2 * band_reach
    targets = adj_cols - (my_index * blocks - band_reach)
    live_mask = jnp.arange(tile_slots)[None, :] < adj_count[:, None]
    chooser = (
        (targets.reshape(-1)[None, :] == jnp.arange(span_blocks)[:, None])
        & live_mask.reshape(-1)[None, :]
    ).astype(jnp.float32)
    summed = jnp.dot(
        chooser, contrib.reshape(blocks * tile_slots, -1), precision=lax.Precision.HIGHEST
    )
    summed = summed.reshape(span_blocks, tile_rows, 2 * chan_width)
    from_prev = shifted(summed[band_reach + blocks :].astype(jnp.bfloat16), "node", 1).astype(
        jnp.float32
    )
    from_next = shifted(summed[:band_reach].astype(jnp.bfloat16), "node", -1).astype(jnp.float32)
    remaining = blocks - band_reach
    middle = summed[band_reach : band_reach + blocks]
    middle = (
        middle
        + jnp.pad(from_prev, ((0, remaining), (0, 0), (0, 0)))
        + jnp.pad(from_next, ((remaining, 0), (0, 0), (0, 0)))
    )
    backprop = middle.astype(jnp.bfloat16).reshape(row_count, 2 * chan_width)
    back_clean = backprop[:, :chan_width]
    back_corrupt = backprop[:, chan_width:]
    my_blocks = my_index * blocks + jnp.arange(blocks)
    all_blocks = jnp.arange(shuffle_from.shape[0])
    one_hot = (shuffle_from[None, :] == my_blocks[:, None]).astype(jnp.int32)
    source_block = jnp.sum(one_hot * all_blocks[None, :], axis=1)
    wanted = (source_block[:, None] * tile_rows + jnp.arange(tile_rows)[None, :]).reshape(-1)
    portion = lax.all_gather(back_corrupt, "node", axis=0, tiled=True)
    inside = (wanted >= 0) & (wanted < portion.shape[0])
    fetched = jnp.take(portion, jnp.clip(wanted, 0, portion.shape[0] - 1), axis=0)
    unshuffled = jnp.where(inside[:, None], fetched, jnp.zeros_like(back_corrupt))
    combined = jnp.concatenate([back_clean, unshuffled], axis=1)
    product = lax.dot_general(
        lax.all_gather(features, "chan", axis=1, tiled=True),
        combined,
        (((0,), (0,)), ((), ())),
        preferred_element_type=jnp.float32,
    )
    partial_w = product[:, :chan_width] + product[:, chan_width:]
    share_rows = partial_w.shape[0] // dev_count
    summed_w = lax.psum(partial_w.astype(jnp.bfloat16), "node").astype(jnp.float32)
    grad_weight = lax.dynamic_slice_in_dim(summed_w, my_index * share_rows, share_rows, 0)
    portion = lax.all_gather(weight, "node", axis=0, tiled=True)
    doubled = jnp.concatenate([portion, portion], axis=1)
    partial_x = lax.dot_general(
        combined, doubled, (((1,), (1,)), ((), ())), preferred_element_type=jnp.float32
    )
    grad_features = lax.psum_scatter(
        partial_x.astype(jnp.bfloat16), "chan", scatter_dimension=1, tiled=True
    )
    return (grad_weight, grad_features)


def solution(mesh):
    placed = (
        P("node", "chan"),
        P("node", "chan"),
        P("node", "chan"),
        P("node", "chan"),
        P("node", "chan"),
        P("node", "chan"),
        P("chan"),
        P("node", None, None, None),
        P("node", None),
        P("node"),
        P(),
    )
    return jax.shard_map(
        local,
        mesh=mesh,
        in_specs=placed,
        out_specs=(P("node", "chan"), P("node", "chan")),
        check_vma=False,
    )
```

profile of v0, /device:TPU:2, one launch (start us, length us, event | category | flops | bytes accessed | tf_op | source)
XLA Modules:
  0.0 460.4 jit_solution(3532302501971480463)
XLA Ops:
  7.2 1.4 copy.28
  8.6 1.2 copy.29
  9.8 1.9 copy.30
  11.7 1.9 copy.31
  13.6 1.5 multiply_convert_fusion.1
  15.2 0.3 pad_maximum_fusion
  15.4 2.9 convolution_bitcast_fusion
  18.3 5.7 %copy.33 = f32[14,5,128,128]{3,2,1,0:T(8,128)} copy(f32[14,5,128,128]{2,3,1,0:T(8,128)} %convolution_bitcast_fusion) | data formatting | bytes 9175040 | tf_op jit(solution)/shard_map/bkpq,bpc->bkqc/dot_general | solution.py:43
  24.1 2.9 pad.25
  27.0 4.9 %copy.38 = f32[9,8,128,128]{3,1,2,0:T(8,128)} copy(f32[9,8,128,128]{3,2,1,0:T(8,128)S(1)} %bitcast.49) | data formatting | bytes 9437184
  31.9 0.1 copy.27
  32.2 0.1 lt.58
  32.3 4.1 fusion.24
  36.5 3.5 collective-permute-start
  40.0 4.5 collective-permute-start.1
  44.6 0.2 copy.39
  44.8 1.5 collective-permute-done.1
  46.4 1.0 fusion.23
  47.4 0.7 all-gather.5.cloned.1.call-update
  48.2 50.6 %all_gather.11 = bf16[1024,64]{1,0:T(8,128)(2,1)S(1)} all-gather(bf16[32,64]{1,0:T(8,128)(2,1)S(1)} %copy-done.1), channel_id=1, replica_groups=mesh['node'=32,'chan'=16] {'node'}, dimensions={0}, use_global_device_ids=true | all-gather | bytes 135168 | tf_op jit(solution)/shard_map/all_gather | solution.py:89
  98.8 0.2 select_reduce_fusion
  99.3 86.6 %all-gather.3.cloned.1.call-done = bf16[57344,64]{1,0:T(8,128)(2,1)} async-done(((bf16[1792,64]{1,0:T(8,128)(2,1)}), bf16[57344,64]{1,0:T(8,128)(2,1)}) %all-gather.3.cloned.1.call-update) | async-done | bytes 7340048 | tf_op jit(solution)/shard_map/all_gather | solution.py:74
  185.9 11.3 %gather_fusion = bf16[1792,64]{1,0:T(8,128)(2,1)} fusion(bf16[57344,64]{1,0:T(8,128)(2,1)} %all-gather.3.cloned.1.call-done, s32[2048]{0:T(1024)S(1)} %pad_clamp_fusion), kind=kCustom, calls=%fused_computation | custom fusion | bytes 465920 | tf_op jit(solution)/shard_map/jit(_take)/gather | solution.py:76
  197.1 2.7 select_select_fusion
  199.8 32.0 %all-gather.5.cloned.1.call-done = bf16[1792,1024]{0,1:T(8,128)(2,1)} async-done(((bf16[1792,64]{0,1:T(8,128)(2,1)}), bf16[1792,1024]{0,1:T(8,128)(2,1)}) %all-gather.5.cloned.1.call-update) | async-done | bytes 3670032 | tf_op jit(solution)/shard_map/all_gather | solution.py:80
  231.8 3.7 convolution_bitcast_fusion.1
  235.5 0.7 fusion.2
  236.2 3.0 convolution_convert_fusion
  239.3 147.1 %all-reduce.4.cloned.1.call-done = bf16[1024,64]{0,1:T(8,128)(2,1)} async-done(((bf16[1024,64]{0,1:T(8,128)(2,1)}), bf16[1024,64]{0,1:T(8,128)(2,1)}) %all-reduce.4.cloned.1.call-update) | async-done | bytes 131088 | tf_op jit(solution)/shard_map/psum | solution.py:87
  386.4 0.8 dynamic-slice_convert_fusion
  387.2 0.7 copy.34
  387.9 66.0 %reduce-scatter.2.cloned.1.call-done = bf16[1792,64]{0,1:T(8,128)(2,1)} async-done(((bf16[1792,1024]{0,1:T(8,128)(2,1)}), bf16[1792,64]{0,1:T(8,128)(2,1)}) %reduce-scatter.2.cloned.1.call-update) | async-done | bytes 229392 | tf_op jit(solution)/shard_map/reduce_scatter | solution.py:94
  (33 shorter events, 0.9 us)
Async XLA Ops:
  7.2 8.3 %copy-start = (bf16[14,5,128,128]{3,2,1,0:T(8,128)(2,1)S(1)}, bf16[14,5,128,128]{3,2,1,0:T(8,128)(2,1)}, u32[]{:S(2)}) copy-start(bf16[14,5,128,128]{3,2,1,0:T(8,128)(2,1)} %param.18) | copy-start | bytes 6881284
  7.2 178.7 %all-gather.3.cloned.1.call-start = ((), (), s32[]{:S(2)}) async-start(), calls=%async_computation.1 | async-start | bytes 15138816 | tf_op jit(solution)/shard_map/all_gather | solution.py:74
  27.0 4.9 %copy-start.2 = (s32[14,5]{0,1:T(8,128)S(1)}, s32[14,5]{0,1:T(8,128)}, u32[]{:S(2)}) copy-start(s32[14,5]{0,1:T(8,128)} %param.19) | copy-start | bytes 844
  27.0 5.1 %copy-start.4 = (s32[14]{0:T(128)S(1)}, s32[14]{0:T(128)}, u32[]{:S(2)}) copy-start(s32[14]{0:T(128)} %param.20) | copy-start | bytes 172
  36.5 8.3 %collective-permute-start = (bf16[2,128,128]{2,1,0:T(8,128)(2,1)S(1)}, bf16[2,128,128]{2,1,0:T(8,128)(2,1)S(1)}, u32[]{:S(2)}, u32[]{:S(2)}) collective-permute-start(bf16[2,128,128]{2,1,0:T(8,128)(2,1)S(1)} %bitcast.56), channel_id=1, source_target_pairs={{0,16},{16,32},{32,48},{48,64},{64,80},{80,96},{96,112},{112,128},... | collective-permute-start | bytes 196616 | tf_op jit(solution)/shard_map/ppermute | solution.py:10
  40.0 6.4 %collective-permute-start.1 = (bf16[2,128,128]{2,1,0:T(8,128)(2,1)S(1)}, bf16[2,128,128]{2,1,0:T(8,128)(2,1)S(1)}, u32[]{:S(2)}, u32[]{:S(2)}) collective-permute-start(bf16[2,128,128]{2,1,0:T(8,128)(2,1)S(1)} %bitcast.57), channel_id=1, source_target_pairs={{16,0},{32,16},{48,32},{64,48},{80,64},{96,80},{112,96},{128,112},... | collective-permute-start | bytes 196616 | tf_op jit(solution)/shard_map/ppermute | solution.py:10
  44.4 3.8 copy-start.1
  44.6 54.2 %copy-start.3 = (s32[448]{0:T(512)S(1)}, s32[448]{0:T(512)}, u32[]{:S(2)}) copy-start(s32[448]{0:T(512)} %param.21) | copy-start | bytes 5380
  47.4 184.4 %all-gather.5.cloned.1.call-start = ((), (), s32[]{:S(2)}) async-start(), calls=%async_computation.2 | async-start | bytes 3899392 | tf_op jit(solution)/shard_map/all_gather | solution.py:80
  48.2 338.2 %all-reduce.4.cloned.1.call-start = ((), (), s32[]{:S(2)}) async-start(), calls=%async_computation.3 | async-start | bytes 262144 | tf_op jit(solution)/shard_map/psum | solution.py:87
  236.2 217.7 %reduce-scatter.2.cloned.1.call-start = ((), (), s32[]{:S(2)}) async-start(), calls=%async_computation.4 | async-start | bytes 3899392 | tf_op jit(solution)/shard_map/reduce_scatter | solution.py:94
Sparse Core Ops, SparseCore 0:
  47.5 138.3 all-gather.2
  188.0 43.7 all-gather.4
  236.3 150.0 all-reduce.3
  389.9 63.8 reduce-scatter.1
where the time goes:
time: 461 us; the launch traced here: 460 us
  waiting for transfers between devices  334 us (72%)
  blocking collectives  50.6 us (11%)
  local copies, waits for them, and re-layouts  33.5 us (7%)
  between operations  14 us (3%)
  matrix products  13.7 us (3%)
  starting transfers between devices  8.11 us (2%)
  other arithmetic  6.56 us (1%)
    psum x1, waiting for transfers between devices, local(): lax.psum(partial_w.astype(jnp.bfloat16), 'node').astype(jnp.float32)  147 us
    all_gather x1, waiting for transfers between devices, local(): portion = lax.all_gather(back_corrupt, 'node', axis=0, tiled=True)  86.6 us
    reduce_scatter x1, waiting for transfers between devices, local(): lax.psum_scatter(partial_x.astype(jnp.bfloat16), 'chan', scatter_dimensio...  66 us
    all_gather x1, blocking collectives, local(): portion = lax.all_gather(weight, 'node', axis=0, tiled=True)  50.6 us
    all_gather x1, waiting for transfers between devices, local(): lax.all_gather(features, 'chan', axis=1, tiled=True)  32 us
    unnamed x21, local copies, waits for them, and re-layouts  15.2 us
    gather x1, local copies, waits for them, and re-layouts, local(): jnp.take(portion, jnp.clip(wanted, 0, portion.shape[0] - 1), axis=0)  11.3 us
  transfers between devices with their start and end apart: 6, of which 5 were waited for; matrix products, arithmetic and copies ran while one was open for 4% of the time, Pallas kernels for 0%

commit v1 on v0

--- a/solution.py
+++ b/solution.py
@@ -2,6 +2,11 @@
 import jax.numpy as jnp
 from jax import lax
 from jax.sharding import PartitionSpec as P
+
+
+def gather_and_add(x, mesh_axis):
+    pieces = lax.all_gather(x, mesh_axis)
+    return jnp.sum(pieces, axis=0)
 
 
 def shifted(value, axis, by):
@@ -84,7 +89,7 @@
     )
     partial_w = product[:, :chan_width] + product[:, chan_width:]
     share_rows = partial_w.shape[0] // dev_count
-    summed_w = lax.psum(partial_w.astype(jnp.bfloat16), "node").astype(jnp.float32)
+    summed_w = gather_and_add(partial_w.astype(jnp.bfloat16), "node").astype(jnp.float32)
     grad_weight = lax.dynamic_slice_in_dim(summed_w, my_index * share_rows, share_rows, 0)
     portion = lax.all_gather(weight, "node", axis=0, tiled=True)
     doubled = jnp.concatenate([portion, portion], axis=1)

time: 461 us -> 395 us (0.86)
  waiting for transfers between devices: 334 us -> 264 us
  local copies, waits for them, and re-layouts: 33.5 us -> 38.2 us
    psum x1 -> x0, waiting for transfers between devices: 147 us -> none  [local(): lax.psum(partial_w.astype(jnp.bfloat16), 'node').astype(jnp.float32)]
    all_gather x1, waiting for transfers between devices: 86.6 us -> 137 us  [local(): portion = lax.all_gather(back_corrupt, 'node', axis=0, tiled=True)]
    all_gather x0 -> x1, waiting for transfers between devices: none -> 32.2 us  [gather_and_add(): pieces = lax.all_gather(x, mesh_axis)]
    reduce_scatter x1, waiting for transfers between devices: 66 us -> 60.4 us  [local(): lax.psum_scatter(partial_x.astype(jnp.bfloat16), 'chan', scatter_dimensio...]
    unnamed x21 -> x22, local copies, waits for them, and re-layouts: 15.2 us -> 19.9 us
  transfers between devices with their start and end apart: 6 -> 6, of which waited for: 5 -> 5; matrix products, arithmetic and copies ran while one was open for 4% -> 6% of each run, Pallas kernels for 0% -> 0%
where the time goes in v1:
time: 395 us; the launch traced here: 394 us
  waiting for transfers between devices  264 us (67%)
  blocking collectives  48.7 us (12%)
  local copies, waits for them, and re-layouts  38.2 us (10%)
  between operations  14 us (4%)
  matrix products  13.7 us (3%)
  starting transfers between devices  8.29 us (2%)
  other arithmetic  7.52 us (2%)
    all_gather x1, waiting for transfers between devices, local(): portion = lax.all_gather(back_corrupt, 'node', axis=0, tiled=True)  137 us
    reduce_scatter x1, waiting for transfers between devices, local(): lax.psum_scatter(partial_x.astype(jnp.bfloat16), 'chan', scatter_dimensio...  60.4 us
    all_gather x1, blocking collectives, local(): portion = lax.all_gather(weight, 'node', axis=0, tiled=True)  48.7 us
    all_gather x1, waiting for transfers between devices, gather_and_add(): pieces = lax.all_gather(x, mesh_axis)  32.2 us
    all_gather x1, waiting for transfers between devices, local(): lax.all_gather(features, 'chan', axis=1, tiled=True)  31.9 us
    unnamed x22, local copies, waits for them, and re-layouts  19.9 us
    gather x1, local copies, waits for them, and re-layouts, local(): jnp.take(portion, jnp.clip(wanted, 0, portion.shape[0] - 1), axis=0)  11.3 us
    ppermute x2, starting transfers between devices, shifted(): return lax.ppermute(value, axis, pairs)  7.95 us
  transfers between devices with their start and end apart: 6, of which 5 were waited for; matrix products, arithmetic and copies ran while one was open for 6% of the time, Pallas kernels for 0%

profile of v1, /device:TPU:2, one launch (start us, length us, event | category | flops | bytes accessed | tf_op | source)
XLA Modules:
  0.0 394.5 jit_solution(7482161486389567624)
XLA Ops:
  7.2 1.4 copy.34
  8.6 1.2 copy.35
  9.8 1.9 copy.36
  11.7 1.9 copy.37
  13.6 1.5 multiply_convert_fusion.1
  15.2 0.3 pad_maximum_fusion
  15.4 2.9 convolution_bitcast_fusion
  18.3 5.7 %copy.39 = f32[14,5,128,128]{3,2,1,0:T(8,128)} copy(f32[14,5,128,128]{2,3,1,0:T(8,128)} %convolution_bitcast_fusion) | data formatting | bytes 9175040 | tf_op jit(solution)/shard_map/bkpq,bpc->bkqc/dot_general | solution.py:48
  24.1 2.9 pad.25
  27.0 4.9 %copy.44 = f32[9,8,128,128]{3,1,2,0:T(8,128)} copy(f32[9,8,128,128]{3,2,1,0:T(8,128)S(1)} %bitcast.54) | data formatting | bytes 9437184
  32.3 4.1 %fusion.24 = (bf16[18,16384]{1,0:T(8,128)(2,1)S(1)}, f32[18,16384]{1,0:T(8,128)S(1)}) fusion(f32[70,16384]{1,0:T(8,128)} %bitcast.55, s32[70]{0:T(128)S(1)} %eq.28, pred[70]{0:T(512)(128)(4,1)S(1)} %lt.58), kind=kOutput, calls=%fused_computation.50 | convolution fusion | flops 248023520 | bytes 6357342 | tf_op jit(solution)/shard_map/dot_general | solution.py:56
  36.5 3.5 collective-permute-start
  40.0 4.5 %collective-permute-start.1 = (bf16[2,128,128]{2,1,0:T(8,128)(2,1)S(1)}, bf16[2,128,128]{2,1,0:T(8,128)(2,1)S(1)}, u32[]{:S(2)}, u32[]{:S(2)}) collective-permute-start(bf16[2,128,128]{2,1,0:T(8,128)(2,1)S(1)} %bitcast.63), channel_id=1, source_target_pairs={{16,0},{32,16},{48,32},{64,48},{80,64},{96,80},{112,96},{128,112},... | collective-permute-start | bytes 196616 | tf_op jit(solution)/shard_map/ppermute | solution.py:15
  44.6 0.2 copy.45
  44.8 1.6 collective-permute-done.1
  46.4 1.0 fusion.23
  47.5 0.7 all-gather.7.cloned.1.call-update
  48.2 0.2 all-gather.9.cloned.1.call-start
  48.4 0.2 select_reduce_fusion
  48.9 137.2 %all-gather.5.cloned.1.call-done = bf16[57344,64]{1,0:T(8,128)(2,1)} async-done(((bf16[1792,64]{1,0:T(8,128)(2,1)}), bf16[57344,64]{1,0:T(8,128)(2,1)}) %all-gather.5.cloned.1.call-update) | async-done | bytes 7340048 | tf_op jit(solution)/shard_map/all_gather | solution.py:79
  186.1 11.3 %gather_fusion = bf16[1792,64]{1,0:T(8,128)(2,1)} fusion(bf16[57344,64]{1,0:T(8,128)(2,1)} %all-gather.5.cloned.1.call-done, s32[2048]{0:T(1024)S(1)} %pad_clamp_fusion), kind=kCustom, calls=%fused_computation | custom fusion | bytes 465920 | tf_op jit(solution)/shard_map/jit(_take)/gather | solution.py:81
  197.4 2.7 select_select_fusion
  200.1 31.9 %all-gather.7.cloned.1.call-done = bf16[1792,1024]{0,1:T(8,128)(2,1)} async-done(((bf16[1792,64]{0,1:T(8,128)(2,1)}), bf16[1792,1024]{0,1:T(8,128)(2,1)}) %all-gather.7.cloned.1.call-update) | async-done | bytes 3670032 | tf_op jit(solution)/shard_map/all_gather | solution.py:85
  232.0 3.7 convolution_bitcast_fusion.1
  235.7 0.7 fusion.2
  236.5 48.7 %all_gather.19 = bf16[1024,64]{1,0:T(8,128)(2,1)S(1)} all-gather(bf16[32,64]{1,0:T(8,128)(2,1)S(1)} %copy-done.1), channel_id=1, replica_groups=mesh['node'=32,'chan'=16] {'node'}, dimensions={0}, use_global_device_ids=true | all-gather | bytes 135168 | tf_op jit(solution)/shard_map/all_gather | solution.py:94
  285.2 3.0 convolution_convert_fusion
  288.2 32.2 %all-gather.9.cloned.1.call-done = bf16[32768,64]{0,1:T(8,128)(2,1)} async-done(((bf16[1024,64]{0,1:T(8,128)(2,1)}), bf16[32768,64]{0,1:T(8,128)(2,1)}) %all-gather.9.cloned.1.call-update) | async-done | bytes 4194320 | tf_op jit(solution)/shard_map/all_gather | solution.py:8
  320.5 4.6 %copy.49 = bf16[8,8,32,1024]{3,2,1,0:T(8,128)(2,1)S(1)} copy(bf16[8,8,32,1024]{3,1,2,0:T(8,128)(2,1)} %bitcast.57) | data formatting | bytes 8388608
  325.1 1.7 bitcast_reduce_fusion
  326.9 0.7 copy.40
  327.5 60.4 %reduce-scatter.2.cloned.1.call-done = bf16[1792,64]{0,1:T(8,128)(2,1)} async-done(((bf16[1792,1024]{0,1:T(8,128)(2,1)}), bf16[1792,64]{0,1:T(8,128)(2,1)}) %reduce-scatter.2.cloned.1.call-update) | async-done | bytes 229392 | tf_op jit(solution)/shard_map/reduce_scatter | solution.py:99
  (35 shorter events, 1.2 us)
Async XLA Ops:
  7.2 8.3 %copy-start = (bf16[14,5,128,128]{3,2,1,0:T(8,128)(2,1)S(1)}, bf16[14,5,128,128]{3,2,1,0:T(8,128)(2,1)}, u32[]{:S(2)}) copy-start(bf16[14,5,128,128]{3,2,1,0:T(8,128)(2,1)} %param.18) | copy-start | bytes 6881284
  7.2 179.0 %all-gather.5.cloned.1.call-start = ((), (), s32[]{:S(2)}) async-start(), calls=%async_computation.1 | async-start | bytes 15138816 | tf_op jit(solution)/shard_map/all_gather | solution.py:79
  27.0 4.9 %copy-start.2 = (s32[14,5]{0,1:T(8,128)S(1)}, s32[14,5]{0,1:T(8,128)}, u32[]{:S(2)}) copy-start(s32[14,5]{0,1:T(8,128)} %param.19) | copy-start | bytes 844
  27.0 5.1 %copy-start.4 = (s32[14]{0:T(128)S(1)}, s32[14]{0:T(128)}, u32[]{:S(2)}) copy-start(s32[14]{0:T(128)} %param.20) | copy-start | bytes 172
  36.5 12.0 %copy-start.3 = (s32[448]{0:T(512)S(1)}, s32[448]{0:T(512)}, u32[]{:S(2)}) copy-start(s32[448]{0:T(512)} %param.21) | copy-start | bytes 5380
  36.5 8.3 %collective-permute-start = (bf16[2,128,128]{2,1,0:T(8,128)(2,1)S(1)}, bf16[2,128,128]{2,1,0:T(8,128)(2,1)S(1)}, u32[]{:S(2)}, u32[]{:S(2)}) collective-permute-start(bf16[2,128,128]{2,1,0:T(8,128)(2,1)S(1)} %bitcast.62), channel_id=1, source_target_pairs={{0,16},{16,32},{32,48},{48,64},{64,80},{80,96},{96,112},{112,128},... | collective-permute-start | bytes 196616 | tf_op jit(solution)/shard_map/ppermute | solution.py:15
  40.0 6.4 %collective-permute-start.1 = (bf16[2,128,128]{2,1,0:T(8,128)(2,1)S(1)}, bf16[2,128,128]{2,1,0:T(8,128)(2,1)S(1)}, u32[]{:S(2)}, u32[]{:S(2)}) collective-permute-start(bf16[2,128,128]{2,1,0:T(8,128)(2,1)S(1)} %bitcast.63), channel_id=1, source_target_pairs={{16,0},{32,16},{48,32},{64,48},{80,64},{96,80},{112,96},{128,112},... | collective-permute-start | bytes 196616 | tf_op jit(solution)/shard_map/ppermute | solution.py:15
  47.4 184.6 %all-gather.7.cloned.1.call-start = ((), (), s32[]{:S(2)}) async-start(), calls=%async_computation.2 | async-start | bytes 3899392 | tf_op jit(solution)/shard_map/all_gather | solution.py:85
  48.2 272.3 %all-gather.9.cloned.1.call-start = ((), (), s32[]{:S(2)}) async-start(), calls=%async_computation.4 | async-start | bytes 4325376 | tf_op jit(solution)/shard_map/all_gather | solution.py:8
  197.4 39.1 %copy-start.1 = (bf16[32,64]{1,0:T(8,128)(2,1)S(1)}, bf16[32,64]{1,0:T(8,128)(2,1)}, u32[]{:S(2)}) copy-start(bf16[32,64]{1,0:T(8,128)(2,1)} %param.12) | copy-start | bytes 12292
  236.4 151.5 %reduce-scatter.2.cloned.1.call-start = ((), (), s32[]{:S(2)}) async-start(), calls=%async_computation.3 | async-start | bytes 3899392 | tf_op jit(solution)/shard_map/reduce_scatter | solution.py:99
Sparse Core Ops, SparseCore 0:
  47.5 138.5 all-gather.4
  188.3 43.7 all-gather.6
  236.5 83.8 all-gather.8
  323.7 64.1 reduce-scatter.1
